TPU v7x, 512 devices: a whole 4x8x8 slice. The times are simulated.
512 devices in a mesh: dp: 16 (over x, y_lo), tensor: 32 (over z, y_hi, core).
Axes of the slice: x: 4, y: 8 (y_hi: 2, y_lo: 4; y = y_hi * 4 + y_lo), z: 8, core: 2. Of those that a mesh axis runs over, the one named last changes fastest.
Arguments:
- grads: bfloat16 [16, 32, 16, 53248], P('dp', 'tensor'), may hold values from -6 to 6
- master: float32 [32, 16, 53248], P('tensor', 'dp'), may hold values from -6 to 6
- first_moment: float32 [32, 16, 53248], P('tensor', 'dp'), may hold values from -3 to 3
- second_moment: float32 [32, 16, 53248], P('tensor', 'dp'), may hold values from 0.01 to 1
Outputs:
- new_master: float32 [32, 16, 53248], P('tensor', 'dp')
- new_first: float32 [32, 16, 53248], P('tensor', 'dp')
- new_second: float32 [32, 16, 53248], P('tensor', 'dp')
- served: bfloat16 [512, 53248], P(None, 'tensor')
All inputs are finite; a program needn't handle non-finite values.
Results may differ from a plain program's by a relative error of at most 0.0038.
Values may be sent and summed in bfloat16 or wider, within the bound.
A program may use at most 64 MiB of HBM per device.

v0:
```python
import jax
import jax.numpy as jnp
from jax import lax
from jax.sharding import PartitionSpec as P


def local(grads, master, first_moment, second_moment):
    ranks = lax.axis_size("dp")
    local_half = grads[0, 0]
    pieces = local_half.reshape(ranks, local_half.shape[0] // ranks, local_half.shape[1])
    received = lax.all_to_all(pieces, "dp", split_axis=0, concat_axis=0, tiled=True)
    gradient = jnp.sum(received.astype(jnp.float32), axis=0) / ranks
    new_first = 0.9 * first_moment[0] + 0.1 * gradient
    new_second = 0.95 * second_moment[0] + 0.05 * gradient * gradient
    corr_first = 1.0 - 0.9**10
    corr_second = 1.0 - 0.95**10
    step_size = new_first / corr_first / (jnp.sqrt(new_second / corr_second) + 1e-08)
    old_master = master[0]
    new_master = old_master - 0.5 * (step_size + 0.1 * old_master)
    weights_half = new_master.astype(jnp.bfloat16)
    slab_rows = lax.all_gather(weights_half, "dp", axis=0, tiled=True)
    served = lax.all_to_all(slab_rows, "tensor", split_axis=1, concat_axis=0, tiled=True)
    return (new_master[None], new_first[None], new_second[None], served)


def solution(mesh):
    in_specs = (
        P("dp", "tensor", None, None),
        P("tensor", "dp", None),
        P("tensor", "dp", None),
        P("tensor", "dp", None),
    )
    out_specs = (
        P("tensor", "dp", None),
        P("tensor", "dp", None),
        P("tensor", "dp", None),
        P(None, "tensor"),
    )
    return jax.shard_map(local, mesh=mesh, in_specs=in_specs, out_specs=out_specs, check_vma=False)
```

profile of v0, /device:TPU:32, one launch (start us, length us, event | category | flops | bytes accessed | tf_op | source)
XLA Modules:
  0.0 259.2 jit_solution(2006858121926900283)
XLA Ops:
  7.2 0.0 all-gather.3.cloned.1.call-start
  7.2 0.5 broadcast.159
  7.7 3.4 %reduce.2 = bf16[16,53248]{1,0:T(8,128)(2,1)S(1)} reduce(bf16[16,1,53248]{2,0,1:T(8,128)(2,1)} %bitcast.49, bf16[]{:T(256)} %broadcast.159), dimensions={1}, to_apply=%copy.10.reduce_sub_computation | reduce | bytes 3407874 | tf_op jit(solution)/shard_map/reshape;squeeze | solution.py:10
  11.1 1.4 reshape.174
  12.6 46.4 %all_to_all.24 = bf16[16,2,26624]{2,1,0:T(2,128)(2,1)} all-to-all(bf16[16,2,26624]{2,1,0:T(2,128)(2,1)S(1)} %reshape.174), channel_id=1, replica_groups=mesh['dp'=16,'tensor'=32] {'dp'}, dimensions={0} | all-to-all | bytes 3407872 | tf_op jit(solution)/shard_map/all_to_all | solution.py:11
  59.0 8.2 %reshape.175 = bf16[16,1,53248]{2,1,0:T(2,128)(2,1)S(1)} reshape(bf16[16,2,26624]{2,1,0:T(2,128)(2,1)} %all_to_all.24) | data formatting | bytes 3407872
  67.2 0.0 copy-start
  67.2 0.0 copy-start.2
  67.2 0.0 copy-start.4
  67.2 4.3 %convert_reduce_fusion = f32[53248]{0:T(1024)S(1)} fusion(bf16[16,1,53248]{2,1,0:T(2,128)(2,1)S(1)} %reshape.175), kind=kLoop, calls=%fused_computation | loop fusion | flops 1650688 | bytes 1916928 | tf_op jit(solution)/shard_map/reduce_sum | solution.py:12
  71.6 0.0 copy-done
  71.6 0.0 copy-done.2
  71.6 0.0 copy-done.4
  71.6 1.9 convert_bitcast_fusion
  73.5 0.0 all-gather.3.cloned.1.call-update
  73.5 97.4 %all-gather.3.cloned.1.call-done = bf16[16,1,53248]{2,1,0:T(2,128)(2,1)} async-done(((bf16[1,1,53248]{2,1,0:T(2,128)(2,1)}), bf16[16,1,53248]{2,1,0:T(2,128)(2,1)}) %all-gather.3.cloned.1.call-update) | async-done | bytes 1703952 | tf_op jit(solution)/shard_map/all_gather | solution.py:21
  170.9 12.1 %reduce.1 = bf16[16,53248]{1,0:T(8,128)(2,1)S(1)} reduce(bf16[16,1,53248]{2,1,0:T(2,128)(2,1)} %all-gather.3.cloned.1.call-done, bf16[]{:T(256)} %constant.30), dimensions={1}, to_apply=%all-gather.reduce_sub_computation | reduce | bytes 3407874 | tf_op jit(solution)/shard_map/all_gather | solution.py:21
  183.1 1.3 copy.14
  184.4 0.0 copy-start.1
  184.4 0.0 copy-start.3
  184.4 0.0 copy-start.5
  184.4 13.0 %all-to-all-start.1 = ((bf16[16,32,1664]{2,0,1:T(8,128)(2,1)}), bf16[16,32,1664]{2,0,1:T(8,128)(2,1)S(1)}, u32[]{:S(2)}, u32[]{:S(2)}) async-start(bf16[16,32,1664]{2,0,1:T(8,128)(2,1)} %bitcast.42), calls=%async_computation.1 | async-start | bytes 3407872 | tf_op jit(solution)/shard_map/all_to_all | solution.py:22
  197.4 0.0 copy-done.1
  197.4 0.0 copy-done.3
  197.4 0.0 copy-done.5
  197.4 2.1 multiply_subtract_fusion
  199.5 51.6 %all-to-all-done.1 = bf16[16,32,1664]{2,0,1:T(8,128)(2,1)S(1)} async-done(((bf16[16,32,1664]{2,0,1:T(8,128)(2,1)}), bf16[16,32,1664]{2,0,1:T(8,128)(2,1)S(1)}, u32[]{:S(2)}, u32[]{:S(2)}) %all-to-all-start.1) | async-done | bytes 1703968 | tf_op jit(solution)/shard_map/all_to_all | solution.py:22
  251.2 1.2 copy.17
  (1 shorter events, 0.0 us)
Async XLA Ops:
  7.2 163.7 %all-gather.3.cloned.1.call-start = ((), (), s32[]{:S(2)}) async-start(), calls=%async_computation.2 | async-start | bytes 3620864 | tf_op jit(solution)/shard_map/all_gather | solution.py:21
  67.2 4.4 %copy-start = (f32[1,1,53248]{2,1,0:T(1,128)S(1)}, f32[1,1,53248]{2,1,0:T(1,128)}, u32[]{:S(2)}) copy-start(f32[1,1,53248]{2,1,0:T(1,128)} %param.5) | copy-start | bytes 638980
  67.2 4.4 %copy-start.2 = (f32[1,1,53248]{2,1,0:T(1,128)S(1)}, f32[1,1,53248]{2,1,0:T(1,128)}, u32[]{:S(2)}) copy-start(f32[1,1,53248]{2,1,0:T(1,128)} %param.6) | copy-start | bytes 638980
  67.2 4.4 %copy-start.4 = (f32[1,1,53248]{2,1,0:T(1,128)S(1)}, f32[1,1,53248]{2,1,0:T(1,128)}, u32[]{:S(2)}) copy-start(f32[1,1,53248]{2,1,0:T(1,128)} %param.7) | copy-start | bytes 638980
  184.4 13.0 %copy-start.1 = (f32[1,1,53248]{2,1,0:T(1,128)S(1)}, f32[1,1,53248]{2,1,0:T(1,128)}, u32[]{:S(2)}) copy-start(f32[1,1,53248]{2,1,0:T(1,128)} %param.5) | copy-start | bytes 638980
  184.4 13.0 %copy-start.3 = (f32[1,1,53248]{2,1,0:T(1,128)S(1)}, f32[1,1,53248]{2,1,0:T(1,128)}, u32[]{:S(2)}) copy-start(f32[1,1,53248]{2,1,0:T(1,128)} %param.6) | copy-start | bytes 638980
  184.4 13.0 %copy-start.5 = (f32[1,1,53248]{2,1,0:T(1,128)S(1)}, f32[1,1,53248]{2,1,0:T(1,128)}, u32[]{:S(2)}) copy-start(f32[1,1,53248]{2,1,0:T(1,128)} %param.7) | copy-start | bytes 638980
  184.4 66.8 %all-to-all-start.1 = ((bf16[16,32,1664]{2,0,1:T(8,128)(2,1)}), bf16[16,32,1664]{2,0,1:T(8,128)(2,1)S(1)}, u32[]{:S(2)}, u32[]{:S(2)}) async-start(bf16[16,32,1664]{2,0,1:T(8,128)(2,1)} %bitcast.42), calls=%async_computation.1 | async-start | bytes 3407872 | tf_op jit(solution)/shard_map/all_to_all | solution.py:22
Sparse Core Ops, SparseCore 0:
  73.6 97.2 all-gather.2
where the time goes:
time: 260 us; the launch traced here: 259 us
  waiting for transfers between devices  149 us (57%)
  blocking collectives  46.4 us (18%)
  other arithmetic  23.9 us (9%)
  between operations  14.1 us (5%)
  starting transfers between devices  13 us (5%)
  local copies, waits for them, and re-layouts  12.6 us (5%)
    all_gather x1, waiting for transfers between devices, local(): slab_rows = lax.all_gather(weights_half, 'dp', axis=0, tiled=True)  97.4 us
    all_to_all x1, waiting for transfers between devices, local(): lax.all_to_all(slab_rows, 'tensor', split_axis=1, concat_axis=0, tiled=True)  51.6 us
    all_to_all x1, blocking collectives, local(): lax.all_to_all(pieces, 'dp', split_axis=0, concat_axis=0, tiled=True)  46.4 us
    all_to_all x1, starting transfers between devices, local(): lax.all_to_all(slab_rows, 'tensor', split_axis=1, concat_axis=0, tiled=True)  13 us
    all_gather x1, other arithmetic, local(): slab_rows = lax.all_gather(weights_half, 'dp', axis=0, tiled=True)  12.1 us
    unnamed x15, local copies, waits for them, and re-layouts  10.8 us
  transfers between devices with their start and end apart: 2, of which 2 were waited for; matrix products, arithmetic and copies ran while one was open for 1% of the time, Pallas kernels for 0%

commit v1 on v0

v1 whole, which is shorter than its diff:
```python
import functools

import jax
import jax.numpy as jnp
from jax import lax
from jax.experimental import pallas as pl
from jax.experimental.pallas import tpu as pltpu
from jax.sharding import PartitionSpec as P

MESH = pl.DeviceIdType.MESH
F32, BF16 = jnp.float32, jnp.bfloat16
CHUNKS = (2, 3, 3, 3, 2)
FIRST = tuple(sum(CHUNKS[:k]) for k in range(len(CHUNKS)))
TILES = sum(CHUNKS)
STAGES = 5


def order():
    n = len(CHUNKS)
    return [
        (stage, step - stage)
        for step in range(n + STAGES)
        for stage in reversed(range(STAGES))
        if 0 <= step - stage < n
    ]


def kernel(
    g_hbm, m_hbm, f_hbm, s_hbm,
    om, of, os, served,
    gv, mv, fv, sv, perm, sendx, recvx, sendy, recvy, fresh, landed, mine, wide,
    load_sem, x_send, x_recv, y_send, y_recv, z_send, z_recv, z_own, w_send, w_recv, a_send, a_recv,
):
    dp, tn = lax.axis_index("dp"), lax.axis_index("tensor")
    x, yl = dp // 4, dp % 4
    z, yh, core = tn // 4, (tn // 2) % 2, tn % 2
    y = yh * 4 + yl
    q = core * 8 + z

    loads = [
        pltpu.make_async_copy(src, dst, load_sem.at[i])
        for i, (src, dst) in enumerate(((g_hbm, gv), (m_hbm, mv), (f_hbm, fv), (s_hbm, sv)))
    ]
    for copy in loads:
        copy.start()

    def device(dx=0, dy=0, dz=0, dc=0):
        to_y = (y + dy) % 8
        return ((x + dx) % 4) * 4 + to_y % 4, ((z + dz) % 8) * 4 + (to_y // 4) * 2 + (core + dc) % 2

    x_peers = [((x + d) % 4, device(dx=d)) for d in range(1, 4)]
    lo_peers = [((yl + d) % 4, (x * 4 + (yl + d) % 4, tn)) for d in range(1, 4)]
    y_peers = [(((y + d) % 8) // 4, device(dy=d)) for d in range(1, 8)]
    z_peers = [
        (((core + dc) % 2) * 8 + (z + dz) % 8, device(dz=dz, dc=dc))
        for dz in range(8) for dc in range(2) if (dz, dc) != (0, 0)
    ]

    barrier = pltpu.get_barrier_semaphore()
    greeted = x_peers + y_peers + z_peers
    for _, peer in greeted:
        pl.semaphore_signal(barrier, inc=1, device_id=peer, device_id_type=MESH)

    row = lax.broadcasted_iota(jnp.int32, (256, 256), 0)
    col = lax.broadcasted_iota(jnp.int32, (256, 256), 1)
    perm[...] = jnp.where(col == (row % 16) * 16 + row // 16, 1.0, 0.0).astype(BF16)

    def swap(rows):
        return jnp.dot(perm[...], rows, preferred_element_type=F32).astype(BF16)

    def remote(src, dst, send, recv, peer):
        return pltpu.make_async_remote_copy(
            src_ref=src, dst_ref=dst, send_sem=send, recv_sem=recv, device_id=peer, device_id_type=MESH
        )

    def tiles(k):
        return range(FIRST[k], FIRST[k] + CHUNKS[k])

    def span(k, per):
        return pl.ds(FIRST[k] * per, CHUNKS[k] * per)

    def x_copies(k):
        return [
            remote(sendx.at[to, :, span(k, 32)], recvx.at[d, :, span(k, 32)], x_send.at[k, d], x_recv.at[k, d], peer)
            for d, (to, peer) in enumerate(x_peers)
        ]

    def y_copies(k):
        return [
            remote(sendy.at[d, span(k, 32)], recvy.at[d, span(k, 32)], y_send.at[k, d], y_recv.at[k, d], peer)
            for d, (_, peer) in enumerate(lo_peers)
        ]

    def z_copies(k):
        return [
            remote(fresh.at[span(k, 1), :, to], landed.at[span(k, 1), :, q], z_send.at[k, d], z_recv.at[k, d], peer)
            for d, (to, peer) in enumerate(z_peers)
        ]

    def z_local(k):
        return pltpu.make_async_copy(fresh.at[span(k, 1), :, q], landed.at[span(k, 1), :, q], z_own.at[k])

    def w_copies(k):
        return [
            remote(mine.at[to, span(k, 16)], wide.at[x, yl, yh, span(k, 16)], w_send.at[k, d], w_recv.at[k, d], peer)
            for d, (to, peer) in enumerate(y_peers)
        ]

    def a_copies(k):
        return [
            remote(wide.at[x, :, :, span(k, 16)], wide.at[x, :, :, span(k, 16)], a_send.at[k, d], a_recv.at[k, d], peer)
            for d, (_, peer) in enumerate(x_peers)
        ]

    def split(k):
        for c in tiles(k):
            halves = []
            for h in range(2):
                columns = [((i % 8 * 4 + h * 2 + i // 8) * TILES + c) * 128 for i in range(16)]
                halves.append(jnp.concatenate([gv[:, at : at + 128] for at in columns], axis=0))
            out = swap(jnp.concatenate(halves, axis=1))
            for j in range(16):
                for h in range(2):
                    sendx[j // 4, j % 4, c * 32 + h * 16 : c * 32 + h * 16 + 16, :] = (
                        out[j * 16 : j * 16 + 16, h * 128 : h * 128 + 128]
                    )

    def over_x(to, rows):
        total = sendx[x, to, rows, :].astype(F32)
        for d in range(3):
            total += recvx[d, to, rows, :].astype(F32)
        return total

    def reduce_x(k):
        for copy in x_copies(k):
            copy.wait_recv()
        for d, (to, _) in enumerate(lo_peers):
            sendy[d, span(k, 32), :] = over_x(to, span(k, 32)).astype(BF16)
        for copy in y_copies(k):
            copy.start()

    def update(k):
        if k == 0:
            for copy in loads[1:]:
                copy.wait()
        for copy in y_copies(k):
            copy.wait_recv()
        for c in tiles(k):
            for h in range(2):
                rows = pl.ds(c * 32 + h * 16, 16)
                total = over_x(yl, rows)
                for d in range(3):
                    total += recvy[d, rows, :].astype(F32)
                total = total / 16
                for e in range(2):
                    gradient = total[e * 8 : e * 8 + 8]
                    at = pl.ds(h * 2 * TILES + e * TILES + c, 8, stride=4 * TILES)
                    first = 0.9 * fv[at, :] + 0.1 * gradient
                    second = 0.95 * sv[at, :] + 0.05 * gradient * gradient
                    of[at, :] = first
                    os[at, :] = second
                    step = first / (1.0 - 0.9**10) / (jnp.sqrt(second / (1.0 - 0.95**10)) + 1e-08)
                    old = mv[at, :]
                    new = old - 0.5 * (step + 0.1 * old)
                    om[at, :] = new
                    for i in range(8):
                        fresh[c, h, e * 8 + i, :, :] = new[i : i + 1]
        z_local(k).start()
        for copy in z_copies(k):
            copy.start()

    def spread(k):
        z_local(k).wait()
        for copy in z_copies(k):
            copy.wait_recv()
        for c in tiles(k):
            for h in range(2):
                block = jnp.concatenate([landed[c, h, i, :, :] for i in range(16)], axis=0).astype(BF16)
                mine[h, c * 16 : c * 16 + 16, :] = block
        for copy in w_copies(k):
            copy.start()
        wide[x, yl, yh, span(k, 16), :] = mine[yh, span(k, 16), :]

    def gather(k):
        for copy in w_copies(k):
            copy.wait_recv()
        for copy in a_copies(k):
            copy.start()

    def serve(k):
        for copy in a_copies(k):
            copy.wait_recv()
        for c in tiles(k):
            halves = [
                jnp.concatenate([wide[j // 4, j % 4, h, c * 16 : c * 16 + 16, :] for j in range(16)], axis=0)
                for h in range(2)
            ]
            out = swap(jnp.concatenate(halves, axis=1))
            for i in range(16):
                for h in range(2):
                    t = i % 8 * 4 + h * 2 + i // 8
                    served[t * 16 : t * 16 + 16, c * 128 : c * 128 + 128] = (
                        out[i * 16 : i * 16 + 16, h * 128 : h * 128 + 128]
                    )

    loads[0].wait()
    split(0)
    pl.semaphore_wait(barrier, len(greeted))
    for copy in x_copies(0):
        copy.start()
    for k in range(1, len(CHUNKS)):
        split(k)
        for copy in x_copies(k):
            copy.start()
    for stage, k in order():
        (reduce_x, update, spread, gather, serve)[stage](k)
    for k in range(len(CHUNKS)):
        for copies in (x_copies, y_copies, z_copies, w_copies, a_copies):
            for copy in copies(k):
                copy.wait_send()


def local(grads, master, first_moment, second_moment):
    n = len(CHUNKS)
    rows = TILES * 32
    dma = pltpu.SemaphoreType.DMA
    vmem = pltpu.VMEM
    flat = jax.ShapeDtypeStruct((rows, 128), F32)
    outs = pl.pallas_call(
        kernel,
        name="refit",
        out_shape=(flat, flat, flat, jax.ShapeDtypeStruct((512, TILES * 128), BF16)),
        in_specs=[pl.BlockSpec(memory_space=pltpu.HBM)] * 4,
        out_specs=[pl.BlockSpec(memory_space=vmem)] * 4,
        scratch_shapes=[
            vmem((16, rows * 128), BF16),
            vmem((rows, 128), F32),
            vmem((rows, 128), F32),
            vmem((rows, 128), F32),
            vmem((256, 256), BF16),
            vmem((4, 4, rows, 128), BF16),
            vmem((3, 4, rows, 128), BF16),
            vmem((3, rows, 128), BF16),
            vmem((3, rows, 128), BF16),
            vmem((TILES, 2, 16, 1, 128), F32),
            vmem((TILES, 2, 16, 1, 128), F32),
            vmem((2, TILES * 16, 128), BF16),
            vmem((4, 4, 2, TILES * 16, 128), BF16),
            dma((4,)),
            dma((n, 3)), dma((n, 3)),
            dma((n, 3)), dma((n, 3)),
            dma((n, 15)), dma((n, 15)), dma((n,)),
            dma((n, 7)), dma((n, 7)),
            dma((n, 3)), dma((n, 3)),
        ],
        compiler_params=pltpu.CompilerParams(
            collective_id=0, has_side_effects=True, vmem_limit_bytes=60 * 2**20
        ),
    )(
        grads.reshape(16, rows * 128),
        master.reshape(rows, 128),
        first_moment.reshape(rows, 128),
        second_moment.reshape(rows, 128),
    )
    new_master, new_first, new_second, served = outs
    shape = master.shape
    return new_master.reshape(shape), new_first.reshape(shape), new_second.reshape(shape), served


def solution(mesh):
    in_specs = (
        P("dp", "tensor", None, None),
        P("tensor", "dp", None),
        P("tensor", "dp", None),
        P("tensor", "dp", None),
    )
    out_specs = (
        P("tensor", "dp", None),
        P("tensor", "dp", None),
        P("tensor", "dp", None),
        P(None, "tensor"),
    )
    return jax.shard_map(local, mesh=mesh, in_specs=in_specs, out_specs=out_specs, check_vma=False)
```

time: 260 us -> 74.9 us (0.29)
  the two profiles are of different devices: /device:TPU:32 before, /device:TPU:8 now
where the time goes in v1:
time: 74.9 us; the launch traced here: 74.7 us
  Pallas kernels  66.4 us (89%)
  local copies, waits for them, and re-layouts  7.65 us (10%)
    pallas_call x1, Pallas kernels, local(): pl.pallas_call(kernel, name='refit', out_shape=(flat, flat, flat, jax.Sha...  66.4 us
    unnamed x4, local copies, waits for them, and re-layouts  7.65 us

profile of v1, /device:TPU:8, one launch (start us, length us, event | category | flops | bytes accessed | tf_op | source)
XLA Modules:
  0.0 74.7 jit_solution(11977754570228014995)
XLA Ops:
  0.6 66.4 %refit.1 = (f32[416,128]{1,0:T(8,128)}, f32[416,128]{1,0:T(8,128)}, f32[416,128]{1,0:T(8,128)}, bf16[512,1664]{1,0:T(8,128)(2,1)}) custom-call(bf16[16,53248]{1,0:T(8,128)(2,1)} %bitcast.7, f32[416,128]{1,0:T(8,128)} %bitcast.8, f32[416,128]{1,0:T(8,128)} %bitcast.9, f32[416,128]{1,0:T(8,128)} %bitcast.10), custom_call_target="tpu_custom_call" | custom-call | tf_op jit(solution)/shard_map/refit/pallas_call | solution.py:229
  67.0 1.6 %copy.12 = f32[1,1,53248]{2,1,0:T(1,128)} copy(f32[1,1,53248]{2,1,0:T(1,128)} %bitcast.13) | data formatting | bytes 425984
  68.7 1.6 %copy.13 = f32[1,1,53248]{2,1,0:T(1,128)} copy(f32[1,1,53248]{2,1,0:T(1,128)} %bitcast.12) | data formatting | bytes 425984
  70.3 1.6 %copy.14 = f32[1,1,53248]{2,1,0:T(1,128)} copy(f32[1,1,53248]{2,1,0:T(1,128)} %bitcast.11) | data formatting | bytes 425984
  71.9 2.8 %copy.15 = bf16[512,1664]{1,0:T(8,128)(2,1)} copy(bf16[512,1664]{1,0:T(8,128)(2,1)} %get-tuple-element.19) | data formatting | bytes 3407872

commit v2 on v1

--- a/solution.py
+++ b/solution.py
@@ -9,27 +9,31 @@
 
 MESH = pl.DeviceIdType.MESH
 F32, BF16 = jnp.float32, jnp.bfloat16
-CHUNKS = (2, 3, 3, 3, 2)
+CHUNKS = (1, 3, 3, 3, 2, 1)
 FIRST = tuple(sum(CHUNKS[:k]) for k in range(len(CHUNKS)))
 TILES = sum(CHUNKS)
-STAGES = 5
+TILE_US = 1.4
+HOPS_US = (2.9, 3.5, 5.7, 5.2, 2.9)
 
 
 def order():
-    n = len(CHUNKS)
-    return [
-        (stage, step - stage)
-        for step in range(n + STAGES)
-        for stage in reversed(range(STAGES))
-        if 0 <= step - stage < n
-    ]
+    ready, link, gathers = [], 0.0, 0.0
+    for k, tiles in enumerate(CHUNKS):
+        link += tiles * TILE_US
+        at = link + HOPS_US[0]
+        for stage in range(4):
+            ready.append((at, stage, k))
+            at += HOPS_US[stage + 1] if stage < 3 else 0.0
+        gathers = max(at, gathers) + tiles * TILE_US
+        ready.append((gathers + HOPS_US[4], 4, k))
+    return [(stage, k) for _, stage, k in sorted(ready)]
 
 
 def kernel(
     g_hbm, m_hbm, f_hbm, s_hbm,
     om, of, os, served,
     gv, mv, fv, sv, perm, sendx, recvx, sendy, recvy, fresh, landed, mine, wide,
-    load_sem, x_send, x_recv, y_send, y_recv, z_send, z_recv, z_own, w_send, w_recv, a_send, a_recv,
+    load_sem, x_send, y_send, z_send, w_send, a_send, x_recv, y_recv, z_recv, w_recv, a_recv,
 ):
     dp, tn = lax.axis_index("dp"), lax.axis_index("tensor")
     x, yl = dp // 4, dp % 4
@@ -37,9 +41,14 @@
     y = yh * 4 + yl
     q = core * 8 + z
 
+    quarter = TILES * 1024
     loads = [
-        pltpu.make_async_copy(src, dst, load_sem.at[i])
-        for i, (src, dst) in enumerate(((g_hbm, gv), (m_hbm, mv), (f_hbm, fv), (s_hbm, sv)))
+        pltpu.make_async_copy(g_hbm.at[:, i : i + quarter], gv.at[:, i : i + quarter], load_sem.at[0])
+        for i in range(0, 4 * quarter, quarter)
+    ]
+    loads += [
+        pltpu.make_async_copy(src, dst, load_sem.at[1 + i])
+        for i, (src, dst) in enumerate(((m_hbm, mv), (f_hbm, fv), (s_hbm, sv)))
     ]
     for copy in loads:
         copy.start()
@@ -81,36 +90,35 @@
 
     def x_copies(k):
         return [
-            remote(sendx.at[to, :, span(k, 32)], recvx.at[d, :, span(k, 32)], x_send.at[k, d], x_recv.at[k, d], peer)
+            remote(sendx.at[to, :, span(k, 32)], recvx.at[d, :, span(k, 32)], x_send, x_recv.at[k], peer)
             for d, (to, peer) in enumerate(x_peers)
         ]
 
     def y_copies(k):
         return [
-            remote(sendy.at[d, span(k, 32)], recvy.at[d, span(k, 32)], y_send.at[k, d], y_recv.at[k, d], peer)
+            remote(sendy.at[d, span(k, 32)], recvy.at[d, span(k, 32)], y_send, y_recv.at[k], peer)
             for d, (_, peer) in enumerate(lo_peers)
         ]
 
     def z_copies(k):
-        return [
-            remote(fresh.at[span(k, 1), :, to], landed.at[span(k, 1), :, q], z_send.at[k, d], z_recv.at[k, d], peer)
-            for d, (to, peer) in enumerate(z_peers)
+        own = pltpu.make_async_copy(fresh.at[span(k, 1), :, q], landed.at[span(k, 1), :, q], z_recv.at[k])
+        return [own] + [
+            remote(fresh.at[span(k, 1), :, to], landed.at[span(k, 1), :, q], z_send, z_recv.at[k], peer)
+            for to, peer in z_peers
         ]
-
-    def z_local(k):
-        return pltpu.make_async_copy(fresh.at[span(k, 1), :, q], landed.at[span(k, 1), :, q], z_own.at[k])
 
     def w_copies(k):
         return [
-            remote(mine.at[to, span(k, 16)], wide.at[x, yl, yh, span(k, 16)], w_send.at[k, d], w_recv.at[k, d], peer)
-            for d, (to, peer) in enumerate(y_peers)
+            remote(mine.at[to, span(k, 16)], wide.at[dp, yh, span(k, 16)], w_send, w_recv.at[k], peer)
+            for to, peer in y_peers
         ]
 
     def a_copies(k):
-        return [
-            remote(wide.at[x, :, :, span(k, 16)], wide.at[x, :, :, span(k, 16)], a_send.at[k, d], a_recv.at[k, d], peer)
-            for d, (_, peer) in enumerate(x_peers)
-        ]
+        own = wide.at[pl.ds(x * 4, 4), :, span(k, 16)]
+        return [remote(own, own, a_send, a_recv.at[k], peer) for _, peer in x_peers]
+
+    def wait(ref, sem):
+        pltpu.make_async_copy(ref, ref, sem).wait()
 
     def split(k):
         for c in tiles(k):
@@ -132,8 +140,7 @@
         return total
 
     def reduce_x(k):
-        for copy in x_copies(k):
-            copy.wait_recv()
+        wait(recvx.at[:, :, span(k, 32)], x_recv.at[k])
         for d, (to, _) in enumerate(lo_peers):
             sendy[d, span(k, 32), :] = over_x(to, span(k, 32)).astype(BF16)
         for copy in y_copies(k):
@@ -141,10 +148,9 @@
 
     def update(k):
         if k == 0:
-            for copy in loads[1:]:
+            for copy in loads[4:]:
                 copy.wait()
-        for copy in y_copies(k):
-            copy.wait_recv()
+        wait(recvy.at[:, span(k, 32)], y_recv.at[k])
         for c in tiles(k):
             for h in range(2):
                 rows = pl.ds(c * 32 + h * 16, 16)
@@ -165,34 +171,29 @@
                     om[at, :] = new
                     for i in range(8):
                         fresh[c, h, e * 8 + i, :, :] = new[i : i + 1]
-        z_local(k).start()
         for copy in z_copies(k):
             copy.start()
 
     def spread(k):
-        z_local(k).wait()
-        for copy in z_copies(k):
-            copy.wait_recv()
+        wait(landed.at[span(k, 1)], z_recv.at[k])
         for c in tiles(k):
             for h in range(2):
                 block = jnp.concatenate([landed[c, h, i, :, :] for i in range(16)], axis=0).astype(BF16)
                 mine[h, c * 16 : c * 16 + 16, :] = block
         for copy in w_copies(k):
             copy.start()
-        wide[x, yl, yh, span(k, 16), :] = mine[yh, span(k, 16), :]
+        wide[dp, yh, span(k, 16), :] = mine[yh, span(k, 16), :]
 
     def gather(k):
-        for copy in w_copies(k):
-            copy.wait_recv()
+        wait(wide.at[0:7, 0, span(k, 16)], w_recv.at[k])
         for copy in a_copies(k):
             copy.start()
 
     def serve(k):
-        for copy in a_copies(k):
-            copy.wait_recv()
+        wait(wide.at[0:12, :, span(k, 16)], a_recv.at[k])
         for c in tiles(k):
             halves = [
-                jnp.concatenate([wide[j // 4, j % 4, h, c * 16 : c * 16 + 16, :] for j in range(16)], axis=0)
+                jnp.concatenate([wide[j, h, c * 16 : c * 16 + 16, :] for j in range(16)], axis=0)
                 for h in range(2)
             ]
             out = swap(jnp.concatenate(halves, axis=1))
@@ -203,7 +204,7 @@
                         out[i * 16 : i * 16 + 16, h * 128 : h * 128 + 128]
                     )
 
-    loads[0].wait()
+    wait(gv, load_sem.at[0])
     split(0)
     pl.semaphore_wait(barrier, len(greeted))
     for copy in x_copies(0):
@@ -214,10 +215,22 @@
             copy.start()
     for stage, k in order():
         (reduce_x, update, spread, gather, serve)[stage](k)
-    for k in range(len(CHUNKS)):
-        for copies in (x_copies, y_copies, z_copies, w_copies, a_copies):
-            for copy in copies(k):
-                copy.wait_send()
+    for ref, sem in (
+        (recvx, x_send),
+        (recvy, y_send),
+        (landed.at[:, :, 0:15], z_send),
+        (wide.at[0:7, 0], w_send),
+        (wide.at[0:12], a_send),
+    ):
+        wait(ref, sem)
+
+
+def store(*refs):
+    copies = [pltpu.make_async_copy(refs[i], refs[4 + i], refs[8].at[i]) for i in (3, 0, 1, 2)]
+    for copy in copies:
+        copy.start()
+    for copy in copies:
+        copy.wait()
 
 
 def local(grads, master, first_moment, second_moment):
@@ -225,11 +238,11 @@
     rows = TILES * 32
     dma = pltpu.SemaphoreType.DMA
     vmem = pltpu.VMEM
-    flat = jax.ShapeDtypeStruct((rows, 128), F32)
+    shapes = ((rows, 128), F32), ((rows, 128), F32), ((rows, 128), F32), ((512, TILES * 128), BF16)
     outs = pl.pallas_call(
         kernel,
         name="refit",
-        out_shape=(flat, flat, flat, jax.ShapeDtypeStruct((512, TILES * 128), BF16)),
+        out_shape=[vmem(*shape) for shape in shapes],
         in_specs=[pl.BlockSpec(memory_space=pltpu.HBM)] * 4,
         out_specs=[pl.BlockSpec(memory_space=vmem)] * 4,
         scratch_shapes=[
@@ -245,23 +258,34 @@
             vmem((TILES, 2, 16, 1, 128), F32),
             vmem((TILES, 2, 16, 1, 128), F32),
             vmem((2, TILES * 16, 128), BF16),
-            vmem((4, 4, 2, TILES * 16, 128), BF16),
+            vmem((16, 2, TILES * 16, 128), BF16),
             dma((4,)),
-            dma((n, 3)), dma((n, 3)),
-            dma((n, 3)), dma((n, 3)),
-            dma((n, 15)), dma((n, 15)), dma((n,)),
-            dma((n, 7)), dma((n, 7)),
-            dma((n, 3)), dma((n, 3)),
+            *([dma] * 5),
+            *([dma((n,))] * 5),
         ],
         compiler_params=pltpu.CompilerParams(
             collective_id=0, has_side_effects=True, vmem_limit_bytes=60 * 2**20
         ),
     )(
-        grads.reshape(16, rows * 128),
-        master.reshape(rows, 128),
-        first_moment.reshape(rows, 128),
-        second_moment.reshape(rows, 128),
+        *(
+            pltpu.with_memory_space_constraint(v, pltpu.HBM)
+            for v in (
+                grads.reshape(16, rows * 128),
+                master.reshape(rows, 128),
+                first_moment.reshape(rows, 128),
+                second_moment.reshape(rows, 128),
+            )
+        )
     )
+    outs = pl.pallas_call(
+        store,
+        name="store",
+        out_shape=[jax.ShapeDtypeStruct(*shape) for shape in shapes],
+        in_specs=[pl.BlockSpec(memory_space=vmem)] * 4,
+        out_specs=[pl.BlockSpec(memory_space=pltpu.HBM)] * 4,
+        scratch_shapes=[dma((4,))],
+        compiler_params=pltpu.CompilerParams(vmem_limit_bytes=2**20),
+    )(*outs)
     new_master, new_first, new_second, served = outs
     shape = master.shape
     return new_master.reshape(shape), new_first.reshape(shape), new_second.reshape(shape), served

time: 74.9 us -> 59.6 us (0.80)
  the two profiles are of different devices: /device:TPU:8 before, /device:TPU:1 now
where the time goes in v2:
time: 59.6 us; the launch traced here: 59.5 us
  Pallas kernels  58.8 us (99%)
  between operations  0.64 us (1%)
    pallas_call x1, Pallas kernels, local(): pl.pallas_call(kernel, name='refit', out_shape=[vmem(*shape) for shape in...  57.4 us
    pallas_call x1, Pallas kernels, local(): pl.pallas_call(store, name='store', out_shape=[jax.ShapeDtypeStruct(*shap...  1.42 us

profile of v2, /device:TPU:1, one launch (start us, length us, event | category | flops | bytes accessed | tf_op | source)
XLA Modules:
  0.0 59.5 jit_solution(18409070722967489443)
XLA Ops:
  0.6 57.4 %refit.1 = (f32[416,128]{1,0:T(8,128)S(1)}, f32[416,128]{1,0:T(8,128)S(1)}, f32[416,128]{1,0:T(8,128)S(1)}, bf16[512,1664]{1,0:T(8,128)(2,1)S(1)}) custom-call(bf16[16,53248]{1,0:T(8,128)(2,1)} %bitcast.7, f32[416,128]{1,0:T(8,128)} %bitcast.8, f32[416,128]{1,0:T(8,128)} %bitcast.9, f32[416,128]{1,0:T(8,128)} %bitcast.10), custom_call_target="tpu_custom_call" | custom-call | tf_op jit(solution)/shard_map/refit/pallas_call | solution.py:242
  58.1 1.4 %store.1 = (f32[416,128]{1,0:T(8,128)}, f32[416,128]{1,0:T(8,128)}, f32[416,128]{1,0:T(8,128)}, bf16[512,1664]{1,0:T(8,128)(2,1)}) custom-call(f32[416,128]{1,0:T(8,128)S(1)} %get-tuple-element.12.refs_0_, f32[416,128]{1,0:T(8,128)S(1)} %get-tuple-element.13.refs_1_, f32[416,128]{1,0:T(8,128)S(1)} %get-tuple-element.14.refs_2_, ...), custom_call_target="tpu_custom_call" | custom-call | tf_op jit(solution)/shard_map/store/pallas_call | solution.py:280

commit v3 on v2

v3 whole, which is shorter than its diff:
```python
import jax
import jax.numpy as jnp
from jax import lax
from jax.experimental import pallas as pl
from jax.experimental.pallas import tpu as pltpu
from jax.sharding import PartitionSpec as P

MESH = pl.DeviceIdType.MESH
F32, BF16 = jnp.float32, jnp.bfloat16
CHUNKS = (1, 2, 2, 2, 2, 2, 2)
DOWN = "BRRABAA"
UP = "ARRRRBA"
FIRST = tuple(sum(CHUNKS[:k]) for k in range(len(CHUNKS)))
TILES = sum(CHUNKS)
ORDER = (
    ("send", 1), ("bsend", 0), ("bsend", 4), ("send", 2), ("send", 3), ("relay", 1), ("bred", 0),
    ("relay", 2), ("send", 5), ("redx", 3), ("redx", 1), ("upd", 0), ("send", 6), ("redx", 2),
    ("bred", 4), ("upd", 3), ("redx", 5), ("upd", 1), ("spread", 0), ("upd", 2), ("redx", 6),
    ("upd", 4), ("upd", 5), ("spread", 3), ("spread", 1), ("upd", 6), ("gath", 0), ("spread", 2),
    ("spread", 4), ("bspread", 5), ("gath", 3), ("serve", 0), ("gath", 1), ("spread", 6),
    ("bgath", 5), ("gath", 2), ("fwd", 3), ("gath", 4), ("fwd", 1), ("fwd", 2), ("gath", 6),
    ("serve", 3), ("fwd", 4), ("serve", 1), ("serve", 2), ("serve", 5), ("serve", 6), ("serve", 4),
)


def kernel(
    g_hbm, m_hbm, f_hbm, s_hbm,
    om, of, os, served,
    gv, mv, fv, sv, perm, parts, got, passed, sums, got_sums, fresh, landed, mine, crossed, wide,
    load_sem, x_send, y_send, z_send, w_send, a_send, x_recv, y_recv, z_recv, w_recv, a_recv, p_recv, f_recv,
):
    dp, tn = lax.axis_index("dp"), lax.axis_index("tensor")
    x, yl = dp // 4, dp % 4
    z, yh, core = tn // 4, (tn // 2) % 2, tn % 2
    y = yh * 4 + yl
    q = core * 8 + z
    right, left, across = (x + 1) % 4, (x + 3) % 4, (x + 2) % 4

    def device(dx=0, dy=0, dz=0, dc=0):
        to_y = (y + dy) % 8
        return ((x + dx) % 4) * 4 + to_y % 4, ((z + dz) % 8) * 4 + (to_y // 4) * 2 + (core + dc) % 2

    to_right, to_left = device(dx=1), device(dx=3)
    x_peers = [((x + d) % 4, device(dx=d)) for d in (2, 1, 3)]
    lo_peers = [((yl + d) % 4, (x * 4 + (yl + d) % 4, tn)) for d in range(1, 4)]
    y_peers = [(((y + d) % 8) // 4, device(dy=d)) for d in (4, 3, 5, 2, 6, 1, 7)]
    z_peers = [
        (((core + dc) % 2) * 8 + (z + dz) % 8, device(dz=dz, dc=dc))
        for dz in (4, 3, 5, 2, 6, 1, 7, 0) for dc in (1, 0) if (dz, dc) != (0, 0)
    ]

    barrier = pltpu.get_barrier_semaphore()
    greeted = x_peers + y_peers + z_peers
    for _, peer in greeted:
        pl.semaphore_signal(barrier, inc=1, device_id=peer, device_id_type=MESH)

    k0 = ORDER[0][1]
    lo, hi = FIRST[k0] * 128, (FIRST[k0] + CHUNKS[k0]) * 128
    width = TILES * 128

    def fetch(first, last, sem):
        for i in range(0, 32 * width, width):
            cut = pl.ds(i + first, last - first)
            pltpu.make_async_copy(g_hbm.at[:, cut], gv.at[:, cut], sem).start()

    fetch(lo, hi, load_sem.at[0])
    if lo:
        fetch(0, lo, load_sem.at[4])
    fetch(hi, width, load_sem.at[4])
    loads = [
        pltpu.make_async_copy(src, dst, load_sem.at[1 + i])
        for i, (src, dst) in enumerate(((m_hbm, mv), (f_hbm, fv), (s_hbm, sv)))
    ]
    for copy in loads:
        copy.start()

    row = lax.broadcasted_iota(jnp.int32, (256, 256), 0)
    col = lax.broadcasted_iota(jnp.int32, (256, 256), 1)
    perm[...] = jnp.where(col == (row % 16) * 16 + row // 16, 1.0, 0.0).astype(BF16)

    def swap(rows):
        return jnp.dot(perm[...], rows, preferred_element_type=F32).astype(BF16)

    def wait(tiles, sem):
        ref = gv.at[:, 0 : tiles * 128]
        pltpu.make_async_copy(ref, ref, sem).wait()

    def remote(src, dst, send, recv, peer):
        pltpu.make_async_remote_copy(
            src_ref=src, dst_ref=dst, send_sem=send, recv_sem=recv, device_id=peer, device_id_type=MESH
        ).start()

    def tiles(k):
        return range(FIRST[k], FIRST[k] + CHUNKS[k])

    def span(k, per):
        return pl.ds(FIRST[k] * per, CHUNKS[k] * per)

    def split(k):
        for c in tiles(k):
            halves = []
            for h in range(2):
                columns = [((i % 8 * 4 + h * 2 + i // 8) * TILES + c) * 128 for i in range(16)]
                halves.append(jnp.concatenate([gv[:, at : at + 128] for at in columns], axis=0))
            out = swap(jnp.concatenate(halves, axis=1))
            for j in range(16):
                for h in range(2):
                    parts[j // 4, j % 4, c * 32 + h * 16 : c * 32 + h * 16 + 16, :] = (
                        out[j * 16 : j * 16 + 16, h * 128 : h * 128 + 128]
                    )

    def send(k):
        split(k)
        if (send.__name__, k) == ORDER[0]:
            pl.semaphore_wait(barrier, len(greeted))
        at = span(k, 32)
        if DOWN[k] == "R":
            remote(parts.at[across, 0:2, at], passed.at[0, :, at], x_send, p_recv.at[k], to_right)
            remote(parts.at[across, 2:4, at], passed.at[1, :, at], x_send, p_recv.at[k], to_left)
            remote(parts.at[right, 2:4, at], got.at[0, 2:4, at], x_send, x_recv.at[k], to_right)
            remote(parts.at[left, 0:2, at], got.at[1, 0:2, at], x_send, x_recv.at[k], to_left)
        else:
            for d, (to, peer) in enumerate(x_peers):
                remote(parts.at[to, :, at], got.at[d, :, at], x_send, x_recv.at[k], peer)

    def relay(k):
        wait(CHUNKS[k] * 8, p_recv.at[k])
        at = span(k, 32)
        for way, (to, first, peer) in enumerate(((right, 0, to_right), (left, 2, to_left))):
            for i in range(2):
                passed[way, i, at, :] = (
                    passed[way, i, at, :].astype(F32) + parts[to, first + i, at, :].astype(F32)
                ).astype(BF16)
            remote(passed.at[way, :, at], got.at[way, first : first + 2, at], x_send, x_recv.at[k], peer)

    def received(k):
        return 2 if DOWN[k] == "R" else 3

    def redx(k):
        wait(CHUNKS[k] * 8 * received(k), x_recv.at[k])
        at = span(k, 32)
        for d, (to, peer) in enumerate(lo_peers):
            total = parts[x, to, at, :].astype(F32)
            for i in range(received(k)):
                total += got[i, to, at, :].astype(F32)
            sums[d, at, :] = total.astype(BF16)
            remote(sums.at[d, at], got_sums.at[d, at], y_send, y_recv.at[k], peer)

    def bsend(k):
        split(k)
        at = span(k, 32)
        for d, (to, peer) in enumerate(lo_peers):
            remote(parts.at[:, to, at], got.at[d, :, at], x_send, x_recv.at[k], peer)

    def bred(k):
        wait(CHUNKS[k] * 24, x_recv.at[k])
        at = span(k, 32)
        for d, (to, peer) in enumerate(x_peers):
            total = parts[to, yl, at, :].astype(F32)
            for i in range(3):
                total += got[i, to, at, :].astype(F32)
            sums[d, at, :] = total.astype(BF16)
            remote(sums.at[d, at], got_sums.at[d, at], y_send, y_recv.at[k], peer)

    def upd(k):
        wait(CHUNKS[k] * 6, y_recv.at[k])
        own = x if DOWN[k] == "B" else yl
        for c in tiles(k):
            for h in range(2):
                rows = pl.ds(c * 32 + h * 16, 16)
                total = parts[x, yl, rows, :].astype(F32)
                for i in range(received(k)):
                    total += got[i, own, rows, :].astype(F32)
                for i in range(3):
                    total += got_sums[i, rows, :].astype(F32)
                total = total / 16
                for e in range(2):
                    gradient = total[e * 8 : e * 8 + 8]
                    at = pl.ds(h * 2 * TILES + e * TILES + c, 8, stride=4 * TILES)
                    first = 0.9 * fv[at, :] + 0.1 * gradient
                    second = 0.95 * sv[at, :] + 0.05 * gradient * gradient
                    of[at, :] = first
                    os[at, :] = second
                    step = first / (1.0 - 0.9**10) / (jnp.sqrt(second / (1.0 - 0.95**10)) + 1e-08)
                    old = mv[at, :]
                    new = old - 0.5 * (step + 0.1 * old)
                    om[at, :] = new
                    for i in range(8):
                        fresh[c, h, e * 8 + i, :, :] = new[i : i + 1]
        at = span(k, 1)
        for to, peer in z_peers:
            remote(fresh.at[at, :, to], landed.at[at, :, q], z_send, z_recv.at[k], peer)
        pltpu.make_async_copy(fresh.at[at, :, q], landed.at[at, :, q], z_recv.at[k]).start()

    def collect(k):
        wait(CHUNKS[k] * 4, z_recv.at[k])
        for c in tiles(k):
            for h in range(2):
                block = jnp.concatenate([landed[c, h, i, :, :] for i in range(16)], axis=0)
                mine[h, c * 16 : c * 16 + 16, :] = block.astype(BF16)

    def spread(k):
        collect(k)
        at = span(k, 16)
        for to, peer in y_peers:
            remote(mine.at[to, at], wide.at[x, yl, yh, at], w_send, w_recv.at[k], peer)
        pltpu.make_async_copy(mine.at[yh, at], wide.at[x, yl, yh, at], w_recv.at[k]).start()

    def gath(k):
        wait(CHUNKS[k] * 8, w_recv.at[k])
        own = wide.at[x, :, :, span(k, 16)]
        for peer in (to_right, to_left) if UP[k] == "R" else [peer for _, peer in x_peers]:
            remote(own, own, a_send, a_recv.at[k], peer)

    def fwd(k):
        wait(CHUNKS[k] * 16, a_recv.at[k])
        for source, first, peer in ((left, 0, to_right), (right, 2, to_left)):
            block = wide.at[source, first : first + 2, :, span(k, 16)]
            remote(block, block, a_send, f_recv.at[k], peer)

    def bspread(k):
        collect(k)
        at = span(k, 16)
        for _, peer in x_peers:
            remote(mine.at[:, at], crossed.at[x, :, at], w_send, w_recv.at[k], peer)
        pltpu.make_async_copy(mine.at[:, at], crossed.at[x, :, at], w_recv.at[k]).start()

    def bgath(k):
        wait(CHUNKS[k] * 8, w_recv.at[k])
        at = span(k, 16)
        for to, peer in y_peers:
            remote(crossed.at[:, to, at], wide.at[:, yl, yh, at], a_send, a_recv.at[k], peer)
        pltpu.make_async_copy(crossed.at[:, yh, at], wide.at[:, yl, yh, at], a_recv.at[k]).start()

    def serve(k):
        if UP[k] == "R":
            wait(CHUNKS[k] * 8, f_recv.at[k])
        else:
            wait(CHUNKS[k] * (32 if UP[k] == "B" else 24), a_recv.at[k])
        for c in tiles(k):
            halves = [
                jnp.concatenate([wide[j // 4, j % 4, h, c * 16 : c * 16 + 16, :] for j in range(16)], axis=0)
                for h in range(2)
            ]
            out = swap(jnp.concatenate(halves, axis=1))
            for i in range(16):
                for h in range(2):
                    t = i % 8 * 4 + h * 2 + i // 8
                    served[t * 16 : t * 16 + 16, c * 128 : c * 128 + 128] = (
                        out[i * 16 : i * 16 + 16, h * 128 : h * 128 + 128]
                    )

    stages = {
        f.__name__: f for f in (send, relay, redx, bsend, bred, upd, spread, gath, fwd, bspread, bgath, serve)
    }
    wait(CHUNKS[k0] * 32, load_sem.at[0])
    for i, (stage, k) in enumerate(ORDER):
        if i == 1:
            wait((TILES - CHUNKS[k0]) * 32, load_sem.at[4])
        if stage == "upd" and "upd" not in [name for name, _ in ORDER[:i]]:
            for copy in loads:
                copy.wait()
        stages[stage](k)

    crosswise = sum(c for c, kind in zip(CHUNKS, UP) if kind == "B")
    straight = TILES - crosswise
    wait(TILES * 24, x_send)
    wait(TILES * 6, y_send)
    sent = landed.at[:, :, 0:15]
    pltpu.make_async_copy(sent, sent, z_send).wait()
    wait(straight * 7 + crosswise * 6, w_send)
    wait(straight * 24 + crosswise * 28, a_send)


def store(*refs):
    copies = [pltpu.make_async_copy(refs[i], refs[4 + i], refs[8].at[i]) for i in (3, 0, 1, 2)]
    for copy in copies:
        copy.start()
    for copy in copies:
        copy.wait()


def local(grads, master, first_moment, second_moment):
    n = len(CHUNKS)
    rows = TILES * 32
    dma = pltpu.SemaphoreType.DMA
    vmem = pltpu.VMEM
    shapes = ((rows, 128), F32), ((rows, 128), F32), ((rows, 128), F32), ((512, TILES * 128), BF16)
    outs = pl.pallas_call(
        kernel,
        name="refit",
        out_shape=[vmem(*shape) for shape in shapes],
        in_specs=[pl.BlockSpec(memory_space=pltpu.HBM)] * 4,
        out_specs=[pl.BlockSpec(memory_space=vmem)] * 4,
        scratch_shapes=[
            vmem((16, rows * 128), BF16),
            vmem((rows, 128), F32),
            vmem((rows, 128), F32),
            vmem((rows, 128), F32),
            vmem((256, 256), BF16),
            vmem((4, 4, rows, 128), BF16),
            vmem((3, 4, rows, 128), BF16),
            vmem((2, 2, rows, 128), BF16),
            vmem((3, rows, 128), BF16),
            vmem((3, rows, 128), BF16),
            vmem((TILES, 2, 16, 1, 128), F32),
            vmem((TILES, 2, 16, 1, 128), F32),
            vmem((2, TILES * 16, 128), BF16),
            vmem((4, 2, TILES * 16, 128), BF16),
            vmem((4, 4, 2, TILES * 16, 128), BF16),
            dma((5,)),
            *([dma] * 5),
            *([dma((n,))] * 7),
        ],
        compiler_params=pltpu.CompilerParams(
            collective_id=0, has_side_effects=True, vmem_limit_bytes=60 * 2**20
        ),
    )(
        *(
            pltpu.with_memory_space_constraint(v, pltpu.HBM)
            for v in (
                grads.reshape(16, rows * 128),
                master.reshape(rows, 128),
                first_moment.reshape(rows, 128),
                second_moment.reshape(rows, 128),
            )
        )
    )
    outs = pl.pallas_call(
        store,
        name="store",
        out_shape=[jax.ShapeDtypeStruct(*shape) for shape in shapes],
        in_specs=[pl.BlockSpec(memory_space=vmem)] * 4,
        out_specs=[pl.BlockSpec(memory_space=pltpu.HBM)] * 4,
        scratch_shapes=[dma((4,))],
        compiler_params=pltpu.CompilerParams(vmem_limit_bytes=2**20),
    )(*outs)
    new_master, new_first, new_second, served = outs
    shape = master.shape
    return new_master.reshape(shape), new_first.reshape(shape), new_second.reshape(shape), served


def solution(mesh):
    in_specs = (
        P("dp", "tensor", None, None),
        P("tensor", "dp", None),
        P("tensor", "dp", None),
        P("tensor", "dp", None),
    )
    out_specs = (
        P("tensor", "dp", None),
        P("tensor", "dp", None),
        P("tensor", "dp", None),
        P(None, "tensor"),
    )
    return jax.shard_map(local, mesh=mesh, in_specs=in_specs, out_specs=out_specs, check_vma=False)
```

time: 59.6 us -> 53.6 us (0.90)
  Pallas kernels: 58.8 us -> 52.8 us
    pallas_call x1, Pallas kernels: 57.4 us -> 51.4 us  [local(): pl.pallas_call(kernel, name='refit', out_shape=[vmem(*shape) for shape in...]
where the time goes in v3:
time: 53.6 us; the launch traced here: 53.4 us
  Pallas kernels  52.8 us (99%)
  between operations  0.64 us (1%)
    pallas_call x1, Pallas kernels, local(): pl.pallas_call(kernel, name='refit', out_shape=[vmem(*shape) for shape in...  51.4 us
    pallas_call x1, Pallas kernels, local(): pl.pallas_call(store, name='store', out_shape=[jax.ShapeDtypeStruct(*shap...  1.42 us

profile of v3, /device:TPU:1, one launch (start us, length us, event | category | flops | bytes accessed | tf_op | source)
XLA Modules:
  0.0 53.4 jit_solution(16607923988214569422)
XLA Ops:
  0.6 51.4 %refit.1 = (f32[416,128]{1,0:T(8,128)S(1)}, f32[416,128]{1,0:T(8,128)S(1)}, f32[416,128]{1,0:T(8,128)S(1)}, bf16[512,1664]{1,0:T(8,128)(2,1)S(1)}) custom-call(bf16[16,53248]{1,0:T(8,128)(2,1)} %bitcast.7, f32[416,128]{1,0:T(8,128)} %bitcast.8, f32[416,128]{1,0:T(8,128)} %bitcast.9, f32[416,128]{1,0:T(8,128)} %bitcast.10), custom_call_target="tpu_custom_call" | custom-call | tf_op jit(solution)/shard_map/refit/pallas_call | solution.py:289
  52.0 1.4 %store.1 = (f32[416,128]{1,0:T(8,128)}, f32[416,128]{1,0:T(8,128)}, f32[416,128]{1,0:T(8,128)}, bf16[512,1664]{1,0:T(8,128)(2,1)}) custom-call(f32[416,128]{1,0:T(8,128)S(1)} %get-tuple-element.12.refs_0_, f32[416,128]{1,0:T(8,128)S(1)} %get-tuple-element.13.refs_1_, f32[416,128]{1,0:T(8,128)S(1)} %get-tuple-element.14.refs_2_, ...), custom_call_target="tpu_custom_call" | custom-call | tf_op jit(solution)/shard_map/store/pallas_call | solution.py:329

commit v4 on v3

--- a/solution.py
+++ b/solution.py
@@ -27,8 +27,18 @@
     g_hbm, m_hbm, f_hbm, s_hbm,
     om, of, os, served,
     gv, mv, fv, sv, perm, parts, got, passed, sums, got_sums, fresh, landed, mine, crossed, wide,
-    load_sem, x_send, y_send, z_send, w_send, a_send, x_recv, y_recv, z_recv, w_recv, a_recv, p_recv, f_recv,
+    heard, load_sem, x_send, y_send, z_send, w_send, a_send, x_recv, y_recv, z_recv, w_recv, a_recv, p_recv, f_recv,
 ):
+    k0 = ORDER[0][1]
+    lo, hi = FIRST[k0] * 128, (FIRST[k0] + CHUNKS[k0]) * 128
+    width = TILES * 128
+
+    def fetch(first, last, sem):
+        for i in range(0, 32 * width, width):
+            cut = pl.ds(i + first, last - first)
+            pltpu.make_async_copy(g_hbm.at[:, cut], gv.at[:, cut], sem).start()
+
+    fetch(lo, hi, load_sem.at[0])
     dp, tn = lax.axis_index("dp"), lax.axis_index("tensor")
     x, yl = dp // 4, dp % 4
     z, yh, core = tn // 4, (tn // 2) % 2, tn % 2
@@ -50,20 +60,26 @@
     ]
 
     barrier = pltpu.get_barrier_semaphore()
-    greeted = x_peers + y_peers + z_peers
-    for _, peer in greeted:
+    steps = (1, 7)
+    greeted = [peer for _, peer in x_peers + lo_peers]
+    greeted += [device(dy=d) for d in steps] + [device(dc=1)]
+    greeted += [device(dz=d, dc=dc) for d in steps for dc in range(2)]
+    for peer in greeted:
         pl.semaphore_signal(barrier, inc=1, device_id=peer, device_id_type=MESH)
 
-    k0 = ORDER[0][1]
-    lo, hi = FIRST[k0] * 128, (FIRST[k0] + CHUNKS[k0]) * 128
-    width = TILES * 128
-
-    def fetch(first, last, sem):
-        for i in range(0, 32 * width, width):
-            cut = pl.ds(i + first, last - first)
-            pltpu.make_async_copy(g_hbm.at[:, cut], gv.at[:, cut], sem).start()
-
-    fetch(lo, hi, load_sem.at[0])
+    def hail(turn):
+        for d in ((1, 7), (2, 6))[turn]:
+            pl.semaphore_signal(heard.at[turn, 0], inc=1, device_id=device(dy=d), device_id_type=MESH)
+            pl.semaphore_signal(heard.at[turn, 1], inc=1, device_id=device(dz=d), device_id_type=MESH)
+
+    def hear(turn):
+        for way in range(2):
+            pl.semaphore_wait(heard.at[turn, way], 2)
+
+    row = lax.broadcasted_iota(jnp.int32, (256, 256), 0)
+    col = lax.broadcasted_iota(jnp.int32, (256, 256), 1)
+    perm[...] = jnp.where(col == (row % 16) * 16 + row // 16, 1.0, 0.0).astype(BF16)
+
     if lo:
         fetch(0, lo, load_sem.at[4])
     fetch(hi, width, load_sem.at[4])
@@ -73,10 +89,6 @@
     ]
     for copy in loads:
         copy.start()
-
-    row = lax.broadcasted_iota(jnp.int32, (256, 256), 0)
-    col = lax.broadcasted_iota(jnp.int32, (256, 256), 1)
-    perm[...] = jnp.where(col == (row % 16) * 16 + row // 16, 1.0, 0.0).astype(BF16)
 
     def swap(rows):
         return jnp.dot(perm[...], rows, preferred_element_type=F32).astype(BF16)
@@ -254,10 +266,17 @@
         f.__name__: f for f in (send, relay, redx, bsend, bred, upd, spread, gath, fwd, bspread, bgath, serve)
     }
     wait(CHUNKS[k0] * 32, load_sem.at[0])
+    hailed = [name in ("send", "bsend") for name, _ in ORDER].index(False)
     for i, (stage, k) in enumerate(ORDER):
         if i == 1:
+            hail(0)
             wait((TILES - CHUNKS[k0]) * 32, load_sem.at[4])
-        if stage == "upd" and "upd" not in [name for name, _ in ORDER[:i]]:
+        before = [name for name, _ in ORDER[:i]]
+        if i == hailed:
+            hear(0)
+            hail(1)
+        if stage == "upd" and "upd" not in before:
+            hear(1)
             for copy in loads:
                 copy.wait()
         stages[stage](k)
@@ -308,6 +327,7 @@
             vmem((2, TILES * 16, 128), BF16),
             vmem((4, 2, TILES * 16, 128), BF16),
             vmem((4, 4, 2, TILES * 16, 128), BF16),
+            pltpu.SemaphoreType.REGULAR((2, 2)),
             dma((5,)),
             *([dma] * 5),
             *([dma((n,))] * 7),

time: 53.6 us -> 53.4 us (level)
  no operation moved by 1% of the time
where the time goes in v4:
time: 53.4 us; the launch traced here: 53.2 us
  Pallas kernels  52.5 us (98%)
  between operations  0.64 us (1%)
    pallas_call x1, Pallas kernels, local(): pl.pallas_call(kernel, name='refit', out_shape=[vmem(*shape) for shape in...  51.1 us
    pallas_call x1, Pallas kernels, local(): pl.pallas_call(store, name='store', out_shape=[jax.ShapeDtypeStruct(*shap...  1.42 us

profile of v4, /device:TPU:1, one launch (start us, length us, event | category | flops | bytes accessed | tf_op | source)
XLA Modules:
  0.0 53.2 jit_solution(2864119276932061085)
XLA Ops:
  0.6 51.1 %refit.1 = (f32[416,128]{1,0:T(8,128)S(1)}, f32[416,128]{1,0:T(8,128)S(1)}, f32[416,128]{1,0:T(8,128)S(1)}, bf16[512,1664]{1,0:T(8,128)(2,1)S(1)}) custom-call(bf16[16,53248]{1,0:T(8,128)(2,1)} %bitcast.7, f32[416,128]{1,0:T(8,128)} %bitcast.8, f32[416,128]{1,0:T(8,128)} %bitcast.9, f32[416,128]{1,0:T(8,128)} %bitcast.10), custom_call_target="tpu_custom_call" | custom-call | tf_op jit(solution)/shard_map/refit/pallas_call | solution.py:308
  51.7 1.4 %store.1 = (f32[416,128]{1,0:T(8,128)}, f32[416,128]{1,0:T(8,128)}, f32[416,128]{1,0:T(8,128)}, bf16[512,1664]{1,0:T(8,128)(2,1)}) custom-call(f32[416,128]{1,0:T(8,128)S(1)} %get-tuple-element.12.refs_0_, f32[416,128]{1,0:T(8,128)S(1)} %get-tuple-element.13.refs_1_, f32[416,128]{1,0:T(8,128)S(1)} %get-tuple-element.14.refs_2_, ...), custom_call_target="tpu_custom_call" | custom-call | tf_op jit(solution)/shard_map/store/pallas_call | solution.py:349

commit v5 on v4

--- a/solution.py
+++ b/solution.py
@@ -12,6 +12,8 @@
 UP = "ARRRRBA"
 FIRST = tuple(sum(CHUNKS[:k]) for k in range(len(CHUNKS)))
 TILES = sum(CHUNKS)
+PASSED = [k for k, way in enumerate(DOWN) if way == "R"]
+FORWARDED = [k for k, way in enumerate(UP) if way == "R"]
 ORDER = (
     ("send", 1), ("bsend", 0), ("bsend", 4), ("send", 2), ("send", 3), ("relay", 1), ("bred", 0),
     ("relay", 2), ("send", 5), ("redx", 3), ("redx", 1), ("upd", 0), ("send", 6), ("redx", 2),
@@ -29,16 +31,6 @@
     gv, mv, fv, sv, perm, parts, got, passed, sums, got_sums, fresh, landed, mine, crossed, wide,
     heard, load_sem, x_send, y_send, z_send, w_send, a_send, x_recv, y_recv, z_recv, w_recv, a_recv, p_recv, f_recv,
 ):
-    k0 = ORDER[0][1]
-    lo, hi = FIRST[k0] * 128, (FIRST[k0] + CHUNKS[k0]) * 128
-    width = TILES * 128
-
-    def fetch(first, last, sem):
-        for i in range(0, 32 * width, width):
-            cut = pl.ds(i + first, last - first)
-            pltpu.make_async_copy(g_hbm.at[:, cut], gv.at[:, cut], sem).start()
-
-    fetch(lo, hi, load_sem.at[0])
     dp, tn = lax.axis_index("dp"), lax.axis_index("tensor")
     x, yl = dp // 4, dp % 4
     z, yh, core = tn // 4, (tn // 2) % 2, tn % 2
@@ -67,6 +59,16 @@
     for peer in greeted:
         pl.semaphore_signal(barrier, inc=1, device_id=peer, device_id_type=MESH)
 
+    k0 = ORDER[0][1]
+    lo, hi = FIRST[k0] * 128, (FIRST[k0] + CHUNKS[k0]) * 128
+    width = TILES * 128
+
+    def fetch(first, last, sem):
+        for i in range(0, 32 * width, width):
+            cut = pl.ds(i + first, last - first)
+            pltpu.make_async_copy(g_hbm.at[:, cut], gv.at[:, cut], sem).start()
+
+    fetch(lo, hi, load_sem.at[0])
     def hail(turn):
         for d in ((1, 7), (2, 6))[turn]:
             pl.semaphore_signal(heard.at[turn, 0], inc=1, device_id=device(dy=d), device_id_type=MESH)
@@ -121,14 +123,17 @@
                         out[j * 16 : j * 16 + 16, h * 128 : h * 128 + 128]
                     )
 
+    def enter(k):
+        if k == ORDER[0][1]:
+            pl.semaphore_wait(barrier, len(greeted))
+
     def send(k):
         split(k)
-        if (send.__name__, k) == ORDER[0]:
-            pl.semaphore_wait(barrier, len(greeted))
+        enter(k)
         at = span(k, 32)
         if DOWN[k] == "R":
-            remote(parts.at[across, 0:2, at], passed.at[0, :, at], x_send, p_recv.at[k], to_right)
-            remote(parts.at[across, 2:4, at], passed.at[1, :, at], x_send, p_recv.at[k], to_left)
+            remote(parts.at[across, 0:2, at], passed.at[0, :, at], x_send, p_recv.at[PASSED.index(k)], to_right)
+            remote(parts.at[across, 2:4, at], passed.at[1, :, at], x_send, p_recv.at[PASSED.index(k)], to_left)
             remote(parts.at[right, 2:4, at], got.at[0, 2:4, at], x_send, x_recv.at[k], to_right)
             remote(parts.at[left, 0:2, at], got.at[1, 0:2, at], x_send, x_recv.at[k], to_left)
         else:
@@ -136,7 +141,7 @@
                 remote(parts.at[to, :, at], got.at[d, :, at], x_send, x_recv.at[k], peer)
 
     def relay(k):
-        wait(CHUNKS[k] * 8, p_recv.at[k])
+        wait(CHUNKS[k] * 8, p_recv.at[PASSED.index(k)])
         at = span(k, 32)
         for way, (to, first, peer) in enumerate(((right, 0, to_right), (left, 2, to_left))):
             for i in range(2):
@@ -160,6 +165,7 @@
 
     def bsend(k):
         split(k)
+        enter(k)
         at = span(k, 32)
         for d, (to, peer) in enumerate(lo_peers):
             remote(parts.at[:, to, at], got.at[d, :, at], x_send, x_recv.at[k], peer)
@@ -228,7 +234,7 @@
         wait(CHUNKS[k] * 16, a_recv.at[k])
         for source, first, peer in ((left, 0, to_right), (right, 2, to_left)):
             block = wide.at[source, first : first + 2, :, span(k, 16)]
-            remote(block, block, a_send, f_recv.at[k], peer)
+            remote(block, block, a_send, f_recv.at[FORWARDED.index(k)], peer)
 
     def bspread(k):
         collect(k)
@@ -246,7 +252,7 @@
 
     def serve(k):
         if UP[k] == "R":
-            wait(CHUNKS[k] * 8, f_recv.at[k])
+            wait(CHUNKS[k] * 8, f_recv.at[FORWARDED.index(k)])
         else:
             wait(CHUNKS[k] * (32 if UP[k] == "B" else 24), a_recv.at[k])
         for c in tiles(k):
@@ -330,7 +336,8 @@
             pltpu.SemaphoreType.REGULAR((2, 2)),
             dma((5,)),
             *([dma] * 5),
-            *([dma((n,))] * 7),
+            *([dma((n,))] * 5),
+            dma((max(1, len(PASSED)),)), dma((max(1, len(FORWARDED)),)),
         ],
         compiler_params=pltpu.CompilerParams(
             collective_id=0, has_side_effects=True, vmem_limit_bytes=60 * 2**20

time: 53.4 us -> 53.5 us (level)
  no operation moved by 1% of the time
where the time goes in v5:
time: 53.5 us; the launch traced here: 53 us
  Pallas kernels  52.4 us (98%)
  between operations  0.64 us (1%)
    pallas_call x1, Pallas kernels, local(): pl.pallas_call(kernel, name='refit', out_shape=[vmem(*shape) for shape in...  51 us
    pallas_call x1, Pallas kernels, local(): pl.pallas_call(store, name='store', out_shape=[jax.ShapeDtypeStruct(*shap...  1.42 us

profile of v5, /device:TPU:1, one launch (start us, length us, event | category | flops | bytes accessed | tf_op | source)
XLA Modules:
  0.0 53.0 jit_solution(15681173333588908440)
XLA Ops:
  0.6 51.0 %refit.1 = (f32[416,128]{1,0:T(8,128)S(1)}, f32[416,128]{1,0:T(8,128)S(1)}, f32[416,128]{1,0:T(8,128)S(1)}, bf16[512,1664]{1,0:T(8,128)(2,1)S(1)}) custom-call(bf16[16,53248]{1,0:T(8,128)(2,1)} %bitcast.7, f32[416,128]{1,0:T(8,128)} %bitcast.8, f32[416,128]{1,0:T(8,128)} %bitcast.9, f32[416,128]{1,0:T(8,128)} %bitcast.10), custom_call_target="tpu_custom_call" | custom-call | tf_op jit(solution)/shard_map/refit/pallas_call | solution.py:314
  51.6 1.4 %store.1 = (f32[416,128]{1,0:T(8,128)}, f32[416,128]{1,0:T(8,128)}, f32[416,128]{1,0:T(8,128)}, bf16[512,1664]{1,0:T(8,128)(2,1)}) custom-call(f32[416,128]{1,0:T(8,128)S(1)} %get-tuple-element.12.refs_0_, f32[416,128]{1,0:T(8,128)S(1)} %get-tuple-element.13.refs_1_, f32[416,128]{1,0:T(8,128)S(1)} %get-tuple-element.14.refs_2_, ...), custom_call_target="tpu_custom_call" | custom-call | tf_op jit(solution)/shard_map/store/pallas_call | solution.py:356
